TPU v7x, 32 devices: a whole 2x2x4 slice. The times are simulated.
32 devices in a mesh: mem: 4 (over x, core), tile: 8 (over z, y).
Axes of the slice: x: 2, y: 2, z: 4, core: 2. Of those that a mesh axis runs over, the one named last changes fastest.
Arguments:
- background: bfloat16 [512, 4, 8, 1024], P('mem', None, 'tile'), may hold values from -6 to 6
- evolved: bfloat16 [512, 32768], P('mem', 'tile'), may hold values from -6 to 6
- obs_value: bfloat16 [32768], P('tile'), may hold values from -8 to 8
- obs_var: bfloat16 [32768], P('tile'), may hold values from 0.5 to 2
- obs_patch: int32 [32768, 1], P('tile'), may hold values from 0 to 31; in each aligned block of 4096 rows (0 to 4095, 4096 to 8191, ...) at most 256 rows name the same one
- obs_pos: int32 [32768], P('tile'), may hold values from 0 to 127
Outputs:
- analysis: bfloat16 [512, 4, 8, 1024], P('mem', None, 'tile')
Inputs may be any that keep to these rules, and one draw needn't show every extreme that they name: `obs_patch`: in each aligned block of 4096 rows (the observations of one tile index) no patch is named by more than 256 rows, a bound that some block reaches.
All inputs are finite; a program needn't handle non-finite values.
Results may differ from a plain program's by a relative error of at most 0.0065.
Values may be sent and summed in bfloat16 or wider, within the bound.
A program may use at most 64 MiB of HBM per device.

v0:
```python
import math

import jax
import jax.numpy as jnp
from jax import lax
from jax.sharding import PartitionSpec as P

PATCH_CELLS = 128
OBS_PATCH = 1024
ITERS = 4


def with_halo(block, sides, width):
    for axis, dim in sides:
        count = lax.axis_size(axis)
        forward = [(i, i + 1) for i in range(count - 1)]
        forward.append((count - 1, 0))
        backward = [(target, source) for source, target in forward]
        low = lax.ppermute(
            lax.slice_in_dim(block, block.shape[dim] - width, None, axis=dim), axis, forward
        )
        high = lax.ppermute(lax.slice_in_dim(block, 0, width, axis=dim), axis, backward)
        block = jnp.concatenate([low, block, high], axis=dim)
    return block


def localize(position, offset):
    distance = (offset * PATCH_CELLS + position + 0.5 - 0.5 * PATCH_CELLS) / PATCH_CELLS
    return jnp.exp(-2.0 * distance * distance)


def gram_terms(centred, innovation, weight, loc_weight):
    weighted = (centred.astype(jnp.float32) * (weight * loc_weight)[None, :]).astype(jnp.bfloat16)
    gram_mat = lax.dot_general(
        weighted, centred, (((1,), (1,)), ((), ())), preferred_element_type=jnp.float32
    )
    gram_vec = jnp.dot(weighted, innovation, preferred_element_type=jnp.float32)
    return (gram_mat, gram_vec)


def inverse_root(gram_mat):
    mat_size = gram_mat.shape[0]
    identity = jnp.eye(mat_size, dtype=jnp.float32)
    norm_scale = jnp.sqrt(jnp.sum(gram_mat * gram_mat))
    root_up = gram_mat / norm_scale
    root_down = identity
    for sweep_index in range(ITERS):
        middle = 1.5 * identity - 0.5 * jnp.dot(root_down, root_up, precision=lax.Precision.HIGHEST)
        root_up = jnp.dot(root_up, middle, precision=lax.Precision.HIGHEST)
        root_down = jnp.dot(middle, root_down, precision=lax.Precision.HIGHEST)
    return root_down / jnp.sqrt(norm_scale)


def transform(gram_mat, gram_vec):
    mat_size = gram_mat.shape[0]
    identity = jnp.eye(mat_size, dtype=jnp.float32)
    inv_root = inverse_root(gram_mat + (mat_size - 1.0) * identity)
    inner_w = jnp.dot(inv_root, gram_vec, precision=lax.Precision.HIGHEST)
    mean_w = jnp.dot(inv_root, inner_w, precision=lax.Precision.HIGHEST)
    return (math.sqrt(mat_size - 1.0) * inv_root + mean_w[:, None]).astype(jnp.bfloat16)


def update(states, transform_mat):
    members = states.shape[0]
    state_mean = jnp.sum(states.astype(jnp.float32), 0) / members
    deviation = (states.astype(jnp.float32) - state_mean[None, :]).astype(jnp.bfloat16)
    mixed = lax.dot_general(
        transform_mat, deviation, (((0,), (0,)), ((), ())), preferred_element_type=jnp.float32
    )
    return (state_mean[None, :] + mixed).astype(jnp.bfloat16)


def obs_weight(var_row, shifted_row):
    is_live = shifted_row.astype(jnp.float32) > 0.5
    safe_var = jnp.where(is_live, var_row.astype(jnp.float32), 1.0)
    return (jnp.where(is_live, 1.0 / safe_var, 0.0), shifted_row.astype(jnp.float32) - 1.0)


def per_device(background, evolved, obs_value, obs_var, obs_patch, obs_pos):
    mem_count = lax.axis_size("mem")
    tile_count = lax.axis_size("tile")
    patches = mem_count * tile_count
    local_members = evolved.shape[0]
    members = local_members * mem_count
    slot_count = 2 * OBS_PATCH
    capacity = slot_count // tile_count
    target = obs_patch[:, 0]
    onehot = (target[:, None] == jnp.arange(patches, dtype=jnp.int32)[None, :]).astype(jnp.int32)
    slot_rank = jnp.sum(jnp.cumsum(onehot, 0) * onehot, 1) - 1
    slot_place = target * capacity + slot_rank
    send_values = (
        jnp.zeros((local_members, patches * capacity), jnp.bfloat16).at[:, slot_place].set(evolved)
    )
    obs_info = jnp.stack([obs_value, obs_var, (obs_pos + 1).astype(jnp.bfloat16)])
    send_info = jnp.zeros((3, patches * capacity), jnp.bfloat16).at[:, slot_place].set(obs_info)
    got_values, got_info = (
        lax.all_to_all(send_values, ("mem", "tile"), split_axis=1, concat_axis=1, tiled=True),
        lax.all_to_all(send_info, ("mem", "tile"), split_axis=1, concat_axis=1, tiled=True),
    )
    gathered = (
        got_values.reshape(local_members, mem_count, slot_count)
        .transpose(1, 0, 2)
        .reshape(members, slot_count)
    )
    got_info = got_info.reshape(3, mem_count, slot_count)[:, 0]
    obs_mean = jnp.sum(gathered.astype(jnp.float32), 0) / members
    centred = (gathered.astype(jnp.float32) - obs_mean[None, :]).astype(jnp.bfloat16)
    innovation = (got_info[0].astype(jnp.float32) - obs_mean).astype(jnp.bfloat16)
    stacked = jnp.concatenate([centred, innovation[None, :], got_info[1:3]], 0)
    window = with_halo(stacked, ((("mem", "tile"), 1),), slot_count)
    weight, position = obs_weight(window[members + 1], window[members + 2])
    offset = jnp.repeat(jnp.array([-1.0, 0.0, 1.0], jnp.float32), slot_count)
    gram_mat, gram_vec = gram_terms(
        window[:members], window[members], weight, localize(position, offset)
    )
    transform_mat = transform(gram_mat, gram_vec)
    states = lax.all_to_all(background, "mem", split_axis=1, concat_axis=0, tiled=True)
    flat_states = states.reshape(states.shape[0], states.shape[3])
    updated = update(flat_states, transform_mat).reshape(states.shape)
    return lax.all_to_all(updated, "mem", split_axis=0, concat_axis=1, tiled=True)


def solution(mesh):
    return jax.shard_map(
        per_device,
        mesh=mesh,
        in_specs=(
            P("mem", None, "tile", None),
            P("mem", "tile"),
            P("tile"),
            P("tile"),
            P("tile", None),
            P("tile"),
        ),
        out_specs=P("mem", None, "tile", None),
        check_vma=False,
    )
```

profile of v0, /device:TPU:1, one launch (start us, length us, event | category | flops | bytes accessed | tf_op | source)
XLA Modules:
  0.0 287.9 jit_solution(18231845851433670636)
XLA Ops:
  0.8 9.2 %reduce-window.6 = s32[32,32,128]{2,1,0:T(8,128)S(1)} reduce-window(s32[32,32,128]{2,1,0:T(8,128)S(1)} %fusion.22, s32[]{:T(128)} %constant.16.clone.1), window={size=1x1x128 pad=0_0x0_0x127_0}, to_apply=%region_1.2 | reduce-window | flops 16646144 | bytes 1048580 | tf_op jit(solution)/shard_map/reduce-window
  16.7 11.9 %scatter_custom_fusion.1 = bf16[3,8192]{0,1:T(8,128)(2,1)S(1)} fusion(s32[4096]{0:T(1024)S(1)} %bitcast.111, bf16[4096,3]{1,0:T(8,128)(2,1)} %copy.54, bf16[]{:T(256)} %constant.14.clone.1), kind=kCustom, calls=%fused_computation.32 | custom fusion | bytes 49664 | tf_op jit(solution)/shard_map/scatter | solution.py:95
  30.1 7.1 %all-to-all-start.2 = ((bf16[3,32,256]{2,0,1:T(4,128)(2,1)}), bf16[3,32,256]{2,0,1:T(4,128)(2,1)S(1)}, u32[]{:S(2)}, u32[]{:S(2)}) async-start(bf16[3,32,256]{2,0,1:T(4,128)(2,1)} %copy.55), calls=%async_computation.2 | async-start | bytes 131072 | tf_op jit(solution)/shard_map/all_to_all | solution.py:98
  37.9 12.5 %scatter_custom_fusion = bf16[128,8192]{0,1:T(8,128)(2,1)} fusion(s32[4096]{0:T(1024)S(1)} %bitcast.112, bf16[4096,128]{1,0:T(8,128)(2,1)S(1)} %copy.52, bf16[]{:T(256)} %constant.14.clone.1), kind=kCustom, calls=%fused_computation.34 | custom fusion | bytes 2097154 | tf_op jit(solution)/shard_map/scatter | solution.py:92
  50.3 5.8 %all-to-all-start.1 = ((bf16[128,32,256]{0,2,1:T(8,128)(2,1)}), bf16[128,32,256]{0,2,1:T(8,128)(2,1)S(1)}, u32[]{:S(2)}, u32[]{:S(2)}) async-start(bf16[128,32,256]{0,2,1:T(8,128)(2,1)} %bitcast.97), calls=%async_computation.1 | async-start | bytes 4194304 | tf_op jit(solution)/shard_map/all_to_all | solution.py:97
  56.2 49.4 %all-to-all-done.1 = bf16[128,32,256]{0,2,1:T(8,128)(2,1)S(1)} async-done(((bf16[128,32,256]{0,2,1:T(8,128)(2,1)}), bf16[128,32,256]{0,2,1:T(8,128)(2,1)S(1)}, u32[]{:S(2)}, u32[]{:S(2)}) %all-to-all-start.1) | async-done | bytes 2097184 | tf_op jit(solution)/shard_map/all_to_all | solution.py:97
  106.4 2.4 convert_element_type.124
  108.8 5.4 %copy.53 = f32[4,128,2048]{2,1,0:T(8,128)} copy(f32[4,128,2048]{1,2,0:T(8,128)} %bitcast.96) | data formatting | bytes 8388608 | tf_op jit(solution)/shard_map/convert_element_type | solution.py:107
  114.2 2.8 fusion.6
  119.4 3.6 %collective-permute-start.1 = (bf16[515,2048]{1,0:T(8,128)(2,1)}, bf16[515,2048]{1,0:T(8,128)(2,1)}, u32[]{:S(2)}, u32[]{:S(2)}) collective-permute-start(bf16[515,2048]{1,0:T(8,128)(2,1)} %pad_maximum_fusion.1), channel_id=1, source_target_pairs={{1,0},{2,1},{3,2},{4,3},{5,4},{6,5},{7,6},{8,7},{9,8},{10,9},{11,1... | collective-permute-start | bytes 6328328 | tf_op jit(solution)/shard_map/ppermute | solution.py:22
  124.2 5.5 %all-to-all-start = ((bf16[128,4,1,1024]{3,0,2,1:T(8,128)(2,1)}), bf16[128,4,1,1024]{3,0,2,1:T(8,128)(2,1)S(1)}, u32[]{:S(2)}, u32[]{:S(2)}) async-start(bf16[128,4,1,1024]{3,0,2,1:T(8,128)(2,1)} %copy.51), calls=%async_computation | async-start | bytes 2097152 | tf_op jit(solution)/shard_map/all_to_all | solution.py:117
  129.9 13.6 %all-to-all-done = bf16[128,4,1,1024]{3,0,2,1:T(8,128)(2,1)S(1)} async-done(((bf16[128,4,1,1024]{3,0,2,1:T(8,128)(2,1)}), bf16[128,4,1,1024]{3,0,2,1:T(8,128)(2,1)S(1)}, u32[]{:S(2)}, u32[]{:S(2)}) %all-to-all-start) | async-done | bytes 1048608 | tf_op jit(solution)/shard_map/all_to_all | solution.py:117
  144.8 66.4 %collective-permute-done = bf16[515,2048]{1,0:T(8,128)(2,1)} collective-permute-done((bf16[515,2048]{1,0:T(8,128)(2,1)}, bf16[515,2048]{1,0:T(8,128)(2,1)}, u32[]{:S(2)}, u32[]{:S(2)}) %collective-permute-start) | collective-permute-done | bytes 2109472 | tf_op jit(solution)/shard_map/ppermute | solution.py:19
  211.3 2.0 collective-permute-done.1
  213.2 7.2 %pad_maximum_fusion = bf16[515,6144]{1,0:T(8,128)(2,1)S(1)} fusion(bf16[515,2048]{1,0:T(8,128)(2,1)} %collective-permute-done.1, bf16[2,2048]{1,0:T(2,128)(2,1)S(1)} %slice_bitcast_fusion, bf16[1,2048]{1,0:T(2,128)(2,1)S(1)} %fusion.36, bf16[512,2048]{1,0:T(8,128)(2,1)S(1)} %fusion.6, bf16[515,2048]{1,0:T(8,128)(2,1)} %collective-permute-done), kind=kLoop, calls=%fused_computation.5 | loop fusion | flops 31641600 | bytes 12656640 | tf_op jit(solution)/shard_map/concatenate | solution.py:23
  221.6 4.2 %multiply_reduce_fusion = (f32[]{:T(128)}, f32[512,512]{1,0:T(8,128)S(1)}) fusion(bf16[515,6144]{1,0:T(8,128)(2,1)S(1)} %pad_maximum_fusion, f32[6144]{0:T(1024)S(1)} %bitcast.103), kind=kOutput, calls=%fused_computation.31 | convolution fusion | flops 3231973376 | bytes 13656068 | tf_op jit(solution)/shard_map/dot_general | solution.py:34
  227.4 1.9 fusion.23
  230.3 1.9 select_subtract_fusion.2
  234.0 10.6 %fusion.39 = f32[512,512]{1,0:T(8,128)S(1)} fusion(f32[512,512]{1,0:T(8,128)S(1)} %select_subtract_fusion.2, f32[512,512]{1,0:T(8,128)S(1)} %fusion.17), kind=kOutput, calls=%fused_computation.81 | convolution fusion | flops 1610612736 | bytes 3145728 | tf_op jit(solution)/shard_map/dot_general | solution.py:50
  248.4 2.8 fusion.41
  251.2 3.1 %select_subtract_fusion = f32[512,512]{1,0:T(8,128)S(1)} fusion(f32[512,512]{1,0:T(8,128)} %fusion.41, f32[512,512]{1,0:T(8,128)S(1)} %fusion.42), kind=kOutput, calls=%fused_computation.16 | convolution fusion | flops 1611661312 | bytes 3145728 | tf_op jit(solution)/shard_map/dot_general | solution.py:48
  254.3 3.1 %convolution_divide_fusion = f32[512,512]{1,0:T(8,128)S(1)} fusion(f32[512,512]{1,0:T(8,128)S(1)} %select_subtract_fusion, f32[512,512]{1,0:T(8,128)} %fusion.41, f32[]{:T(128)S(6)} %sqrt.7), kind=kOutput, calls=%fused_computation.21 | convolution fusion | flops 1610874880 | bytes 3145732 | tf_op jit(solution)/shard_map/dot_general | solution.py:50
  257.4 4.6 %fusion.12 = f32[512,1]{0,1:T(1,128)S(1)} fusion(f32[6144]{0:T(1024)S(1)} %bitcast.104, bf16[515,6144]{1,0:T(8,128)(2,1)} %copy-done, bf16[515,2048]{1,0:T(8,128)(2,1)} %collective-permute-done.1, bf16[515,2048]{1,0:T(8,128)(2,1)} %collective-permute-done, bf16[2,2048]{1,0:T(2,128)(2,1)S(1)} %slice_bitcast_fusion, bf16[1,2048]{1,0:T(2,128)(2,1)S(1)} %fusion.36, ...), kind=kOutput, calls=%fused_computation.27 | convolution fusion | flops 15790080 | bytes 12687360 | tf_op jit(solution)/shard_map/dot_general | solution.py:37
  267.8 16.7 %all_to_all.45 = bf16[4,2,65536]{2,1,0:T(2,128)(2,1)S(1)} all-to-all(bf16[4,2,65536]{2,1,0:T(2,128)(2,1)S(1)} %reshape.137), channel_id=1, replica_groups=mesh['mem'=4,'tile'=8] {'mem'}, dimensions={0} | all-to-all | bytes 2097152 | tf_op jit(solution)/shard_map/all_to_all | solution.py:120
  (57 shorter events, 33.2 us)
Async XLA Ops:
  10.0 27.2 %copy-start.1 = (bf16[128,4096]{1,0:T(8,128)(2,1)S(1)}, bf16[128,4096]{1,0:T(8,128)(2,1)}, u32[]{:S(2)}) copy-start(bf16[128,4096]{1,0:T(8,128)(2,1)} %param.8) | copy-start | bytes 3145732
  30.1 20.3 %all-to-all-start.2 = ((bf16[3,32,256]{2,0,1:T(4,128)(2,1)}), bf16[3,32,256]{2,0,1:T(4,128)(2,1)S(1)}, u32[]{:S(2)}, u32[]{:S(2)}) async-start(bf16[3,32,256]{2,0,1:T(4,128)(2,1)} %copy.55), calls=%async_computation.2 | async-start | bytes 131072 | tf_op jit(solution)/shard_map/all_to_all | solution.py:98
  50.3 55.3 %all-to-all-start.1 = ((bf16[128,32,256]{0,2,1:T(8,128)(2,1)}), bf16[128,32,256]{0,2,1:T(8,128)(2,1)S(1)}, u32[]{:S(2)}, u32[]{:S(2)}) async-start(bf16[128,32,256]{0,2,1:T(8,128)(2,1)} %bitcast.97), calls=%async_computation.1 | async-start | bytes 4194304 | tf_op jit(solution)/shard_map/all_to_all | solution.py:97
  114.2 8.8 %copy-start.2 = (bf16[128,4,1,1024]{3,1,2,0:T(4,128)(2,1)S(1)}, bf16[128,4,1,1024]{3,1,2,0:T(4,128)(2,1)}, u32[]{:S(2)}) copy-start(bf16[128,4,1,1024]{3,1,2,0:T(4,128)(2,1)} %param.7) | copy-start | bytes 3145732
  117.0 12.8 %copy-start.4 = (f32[3]{0:T(128)S(1)}, f32[3]{0:T(128)}, u32[]{:S(2)}) copy-start(f32[3]{0:T(128)} %constant.56) | copy-start | bytes 40
  118.5 92.7 %collective-permute-start = (bf16[515,2048]{1,0:T(8,128)(2,1)}, bf16[515,2048]{1,0:T(8,128)(2,1)}, u32[]{:S(2)}, u32[]{:S(2)}) collective-permute-start(bf16[515,2048]{1,0:T(8,128)(2,1)} %pad_maximum_fusion.1), channel_id=1, source_target_pairs={{0,1},{1,2},{2,3},{3,4},{4,5},{5,6},{6,7},{7,8},{8,9},{9,10},{10,1... | collective-permute-start | bytes 6328328 | tf_op jit(solution)/shard_map/ppermute | solution.py:19
  119.4 93.9 %collective-permute-start.1 = (bf16[515,2048]{1,0:T(8,128)(2,1)}, bf16[515,2048]{1,0:T(8,128)(2,1)}, u32[]{:S(2)}, u32[]{:S(2)}) collective-permute-start(bf16[515,2048]{1,0:T(8,128)(2,1)} %pad_maximum_fusion.1), channel_id=1, source_target_pairs={{1,0},{2,1},{3,2},{4,3},{5,4},{6,5},{7,6},{8,7},{9,8},{10,9},{11,1... | collective-permute-start | bytes 6328328 | tf_op jit(solution)/shard_map/ppermute | solution.py:22
  124.2 19.2 %all-to-all-start = ((bf16[128,4,1,1024]{3,0,2,1:T(8,128)(2,1)}), bf16[128,4,1,1024]{3,0,2,1:T(8,128)(2,1)S(1)}, u32[]{:S(2)}, u32[]{:S(2)}) async-start(bf16[128,4,1,1024]{3,0,2,1:T(8,128)(2,1)} %copy.51), calls=%async_computation | async-start | bytes 2097152 | tf_op jit(solution)/shard_map/all_to_all | solution.py:117
  220.4 5.3 %copy-start = (bf16[515,6144]{1,0:T(8,128)(2,1)}, bf16[515,6144]{1,0:T(8,128)(2,1)S(1)}, u32[]{:S(2)}) copy-start(bf16[515,6144]{1,0:T(8,128)(2,1)S(1)} %pad_maximum_fusion) | copy-start | bytes 18984964
  257.4 6.8 %copy-start.3 = (bf16[512,1024]{1,0:T(8,128)(2,1)S(1)}, bf16[512,1024]{1,0:T(8,128)(2,1)}, u32[]{:S(2)}) copy-start(bf16[512,1024]{1,0:T(8,128)(2,1)} %fusion.7) | copy-start | bytes 3145732
where the time goes:
time: 293 us; the launch traced here: 288 us
  waiting for transfers between devices  131 us (45%)
  matrix products  42.7 us (15%)
  local copies, waits for them, and re-layouts  41.5 us (14%)
  other arithmetic  31.5 us (11%)
  starting transfers between devices  22.9 us (8%)
  blocking collectives  16.7 us (6%)
    ppermute x1, waiting for transfers between devices, with_halo(): lax.ppermute(lax.slice_in_dim(block, block.shape[dim] - width, None, axis...  66.4 us
    all_to_all x1, waiting for transfers between devices, per_device(): lax.all_to_all(send_values, ('mem', 'tile'), split_axis=1, concat_axis=1,...  49.4 us
    dot_general x4, matrix products, inverse_root(): root_down = jnp.dot(middle, root_down, precision=lax.Precision.HIGHEST)  17.5 us
    all_to_all x1, blocking collectives, per_device(): lax.all_to_all(updated, 'mem', split_axis=0, concat_axis=1, tiled=True)  16.7 us
    all_to_all x1, waiting for transfers between devices, per_device(): lax.all_to_all(background, 'mem', split_axis=1, concat_axis=0, tiled=True)  13.6 us
    scatter x1, local copies, waits for them, and re-layouts, per_device(): jnp.zeros((local_members, patches * capacity), jnp.bfloat16)  12.5 us
    scatter x1, local copies, waits for them, and re-layouts, per_device(): jnp.zeros((3, patches * capacity), jnp.bfloat16).at[:, slot_place]  11.9 us
    another operation x3, other arithmetic  9.62 us
  transfers between devices with their start and end apart: 5, of which 4 were waited for; matrix products, arithmetic and copies ran while one was open for 6% of the time, Pallas kernels for 0%

commit v1 on v0

v1 whole, which is shorter than its diff:
```python
import functools
import math

import jax
import jax.numpy as jnp
from jax import lax
from jax.experimental import pallas as pl
from jax.experimental.pallas import tpu as pltpu
from jax.sharding import PartitionSpec as P

PATCH_CELLS = 128
OBS_PATCH = 1024
INFO = 16
VMEM_LIMIT = 48 * 1024 * 1024
NT = (((1,), (1,)), ((), ()))


def dispatch_kernel(patches, capacity, data_ref, target_ref, out_ref, rank_ref):
    obs = data_ref.shape[1]
    chunk = 256
    upper = (
        lax.broadcasted_iota(jnp.int32, (chunk, chunk), 0)
        <= lax.broadcasted_iota(jnp.int32, (chunk, chunk), 1)
    ).astype(jnp.float32).astype(jnp.bfloat16)
    names = lax.broadcasted_iota(jnp.int32, (patches, chunk), 0)
    carry = jnp.zeros((patches, 1), jnp.float32)
    for start in range(0, obs, chunk):
        hit = names == target_ref[:, start : start + chunk]
        one = jnp.where(hit, 1.0, 0.0)
        run = jnp.dot(one.astype(jnp.bfloat16), upper, preferred_element_type=jnp.float32)
        rank_ref[:, start : start + chunk] = jnp.sum(one * (run + carry), 0, keepdims=True) - 1.0
        carry = carry + jnp.sum(one, 1, keepdims=True)
    slots = lax.broadcasted_iota(jnp.int32, (capacity, obs), 0).astype(jnp.float32)

    def one_patch(patch, _):
        rank = jnp.where(target_ref[...] == patch, rank_ref[...], -1.0)
        pick = jnp.where(slots == rank, 1.0, 0.0).astype(jnp.bfloat16)
        out_ref[patch] = lax.dot_general(
            data_ref[...], pick, NT, preferred_element_type=jnp.float32
        ).astype(jnp.bfloat16)
        return 0

    lax.fori_loop(0, patches, one_patch, 0)


def dispatch(data, target, patches, capacity):
    rows, obs = data.shape
    return pl.pallas_call(
        functools.partial(dispatch_kernel, patches, capacity),
        out_shape=jax.ShapeDtypeStruct((patches, rows, capacity), jnp.bfloat16),
        in_specs=[pl.BlockSpec(memory_space=pltpu.VMEM)] * 2,
        out_specs=pl.BlockSpec(memory_space=pltpu.VMEM),
        scratch_shapes=[pltpu.VMEM((1, obs), jnp.float32)],
        compiler_params=pltpu.CompilerParams(vmem_limit_bytes=VMEM_LIMIT),
    )(data, target)


def gram_kernel(mem_count, tile_count, got_ref, own_ref, next_ref, prev_ref, own_acc, next_acc, prev_acc):
    tile = pl.program_id(0)
    local = got_ref.shape[2] - INFO
    members = local * mem_count
    values = jnp.concatenate(
        [got_ref[m, 0, :local, :].astype(jnp.float32) for m in range(mem_count)], 0
    )
    obs_mean = jnp.sum(values, 0, keepdims=True) / members
    centred = (values - obs_mean).astype(jnp.bfloat16)
    value = got_ref[0, 0, local : local + 1, :].astype(jnp.float32)
    var = got_ref[0, 0, local + 1 : local + 2, :].astype(jnp.float32)
    shifted = got_ref[0, 0, local + 2 : local + 3, :].astype(jnp.float32)
    is_live = shifted > 0.5
    weight = jnp.where(is_live, 1.0 / jnp.where(is_live, var, 1.0), 0.0)
    position = shifted - 1.0
    innovation = (value - obs_mean).astype(jnp.bfloat16).astype(jnp.float32)
    first = lax.broadcasted_iota(jnp.int32, (16, innovation.shape[1]), 0) == 0
    vector_rows = jnp.where(first, innovation, 0.0).astype(jnp.bfloat16)
    left = jnp.concatenate([centred, vector_rows], 0)
    centred_wide = centred.astype(jnp.float32)
    for offset, acc in ((0.0, own_acc), (-1.0, next_acc), (1.0, prev_acc)):
        distance = (offset * PATCH_CELLS + position + 0.5 - 0.5 * PATCH_CELLS) / PATCH_CELLS
        scale = weight * jnp.exp(-2.0 * distance * distance)
        weighted = (centred_wide * scale).astype(jnp.bfloat16)
        term = lax.dot_general(left, weighted, NT, preferred_element_type=jnp.float32)

        @pl.when(tile == 0)
        def _():
            acc[...] = term

        @pl.when(tile > 0)
        def _():
            acc[...] += term

    @pl.when(tile == tile_count - 1)
    def _():
        own_ref[...] = own_acc[...]
        next_ref[...] = next_acc[...].astype(jnp.bfloat16)
        prev_ref[...] = prev_acc[...].astype(jnp.bfloat16)


def gram_terms(got, mem_count, tile_count):
    rows, capacity = got.shape[2:]
    members = (rows - INFO) * mem_count
    shape = (members + 16, members)
    whole = pl.BlockSpec(shape, lambda t: (0, 0))
    return pl.pallas_call(
        functools.partial(gram_kernel, mem_count, tile_count),
        grid=(tile_count,),
        out_shape=[
            jax.ShapeDtypeStruct(shape, jnp.float32),
            jax.ShapeDtypeStruct(shape, jnp.bfloat16),
            jax.ShapeDtypeStruct(shape, jnp.bfloat16),
        ],
        in_specs=[pl.BlockSpec((mem_count, 1, rows, capacity), lambda t: (0, t, 0, 0))],
        out_specs=[whole] * 3,
        scratch_shapes=[pltpu.VMEM(shape, jnp.float32)] * 3,
        compiler_params=pltpu.CompilerParams(vmem_limit_bytes=VMEM_LIMIT),
    )(got)


def split(a):
    high = a.astype(jnp.bfloat16)
    return high, (a - high.astype(jnp.float32)).astype(jnp.bfloat16)


def product(a, b):
    dot = functools.partial(jnp.dot, preferred_element_type=jnp.float32)
    return dot(a[0], b[0]) + (dot(a[0], b[1]) + dot(a[1], b[0]))


def update_kernel(own_ref, low_ref, high_ref, states_ref, out_ref):
    members = own_ref.shape[1]
    total = own_ref[...] + low_ref[...].astype(jnp.float32) + high_ref[...].astype(jnp.float32)
    diagonal = lax.broadcasted_iota(jnp.int32, (members, members), 0) == lax.broadcasted_iota(
        jnp.int32, (members, members), 1
    )
    identity = jnp.where(diagonal, 1.0, 0.0)
    gram_mat = total[:members] + (members - 1.0) * identity
    gram_vec = total[members:]
    norm_scale = jnp.sqrt(jnp.sum(gram_mat * gram_mat, keepdims=True))
    a = gram_mat / norm_scale
    a_pair = split(a)
    square = product(a_pair, a_pair)
    root = (
        2.25 * identity - 2.4375 * a + 1.6875 * square
        + product(split(square), split(0.0625 * square - 0.5625 * a))
    )
    for _ in range(2):
        root_pair = split(root)
        inner = product(a_pair, split(product(root_pair, root_pair)))
        root = 1.5 * root - 0.5 * product(root_pair, split(inner))
    inv_root = root / jnp.sqrt(norm_scale)
    inv_pair = split(inv_root)
    mean_w = product(split(product(split(gram_vec), inv_pair)), inv_pair)[:1]
    transform = (math.sqrt(members - 1.0) * inv_root + mean_w).astype(jnp.bfloat16)
    states = states_ref[...].astype(jnp.float32)
    state_mean = jnp.sum(states, 0, keepdims=True) / members
    deviation = (states - state_mean).astype(jnp.bfloat16)
    mixed = jnp.dot(transform, deviation, preferred_element_type=jnp.float32)
    out_ref[...] = (state_mean + mixed).astype(jnp.bfloat16)


def update(own, low, high, states):
    return pl.pallas_call(
        update_kernel,
        out_shape=jax.ShapeDtypeStruct(states.shape, jnp.bfloat16),
        in_specs=[pl.BlockSpec(memory_space=pltpu.VMEM)] * 4,
        out_specs=pl.BlockSpec(memory_space=pltpu.VMEM),
        compiler_params=pltpu.CompilerParams(vmem_limit_bytes=VMEM_LIMIT),
    )(own, low, high, states)


def per_device(background, evolved, obs_value, obs_var, obs_patch, obs_pos):
    mem_count = lax.axis_size("mem")
    tile_count = lax.axis_size("tile")
    patches = mem_count * tile_count
    local, obs = evolved.shape
    members = local * mem_count
    cells = background.shape[3]
    capacity = 2 * OBS_PATCH // tile_count
    info = jnp.stack([obs_value, obs_var, (obs_pos + 1).astype(jnp.bfloat16)])
    info = jnp.concatenate([info, jnp.zeros((INFO - 3, obs), jnp.bfloat16)], 0)
    data = jnp.concatenate([evolved, info], 0)
    states = background[:, :, 0, :].transpose(1, 0, 2)
    states = lax.all_to_all(states, "mem", split_axis=0, concat_axis=0, tiled=True)
    send = dispatch(data, obs_patch.reshape(1, obs), patches, capacity)
    got = lax.all_to_all(send, ("mem", "tile"), split_axis=0, concat_axis=0, tiled=True)
    got = got.reshape(mem_count, tile_count, local + INFO, capacity)
    own, to_next, to_prev = gram_terms(got, mem_count, tile_count)
    forward = [(i, (i + 1) % patches) for i in range(patches)]
    backward = [(target, source) for source, target in forward]
    low = lax.ppermute(to_next, ("mem", "tile"), forward)
    high = lax.ppermute(to_prev, ("mem", "tile"), backward)
    updated = update(own, low, high, states.reshape(members, cells))
    back = lax.all_to_all(
        updated.reshape(mem_count, local, cells), "mem", split_axis=0, concat_axis=0, tiled=True
    )
    return back.transpose(1, 0, 2).reshape(background.shape)


def solution(mesh):
    return jax.shard_map(
        per_device,
        mesh=mesh,
        in_specs=(
            P("mem", None, "tile", None),
            P("mem", "tile"),
            P("tile"),
            P("tile"),
            P("tile", None),
            P("tile"),
        ),
        out_specs=P("mem", None, "tile", None),
        check_vma=False,
    )
```

time: 293 us -> 172 us (0.59); the launches traced: 288 us -> 170 us
  waiting for transfers between devices: 131 us -> 75.3 us
  Pallas kernels: 0 us -> 49.2 us
  matrix products: 42.7 us -> 0 us
  other arithmetic: 31.5 us -> 0.74 us
  local copies, waits for them, and re-layouts: 41.5 us -> 12.3 us
  starting transfers between devices: 22.9 us -> 15.8 us
    pallas_call x0 -> x3, Pallas kernels: none -> 49.2 us  [the longest x1 26.9 us: dispatch(): pl.pallas_call(functools.partial(dispatch_kernel, patches, capacity), out...]
    ppermute x2, waiting for transfers between devices: 68.4 us -> 21.2 us  [the longest x1 19.3 us: per_device(): low = lax.ppermute(to_next, ('mem', 'tile'), forward)]
    dot_general x16 -> x0, matrix products: 42.7 us -> none  [the longest x4 17.5 us: inverse_root(): root_down = jnp.dot(middle, root_down, precision=lax.Precision.HIGHEST)]
    scatter x2 -> x0, local copies, waits for them, and re-layouts: 24.3 us -> none  [the longest x1 12.5 us: per_device(): jnp.zeros((local_members, patches * capacity), jnp.bfloat16)]
    another operation x4 -> x0, other arithmetic: 9.68 us -> none
    all_to_all x3 -> x2, waiting for transfers between devices: 63 us -> 54 us  [the longest x1 54 us: per_device(): lax.all_to_all(send, ('mem', 'tile'), split_axis=0, concat_axis=0, tiled=...]
    concatenate x2 -> x0, other arithmetic: 8.69 us -> none  [the longest x1 7.18 us: with_halo(): block = jnp.concatenate([low, block, high], axis=dim)]
    convert_element_type x6 -> x1, other arithmetic: 7.9 us -> 0.74 us  [per_device(): info = jnp.stack([obs_value, obs_var, (obs_pos + 1).astype(jnp.bfloat16)])]
  transfers between devices with their start and end apart: 5 -> 4, of which waited for: 4 -> 3; matrix products, arithmetic and copies ran while one was open for 6% -> 1% of each run, Pallas kernels for 0% -> 8%
where the time goes in v1:
time: 172 us; the launch traced here: 170 us
  waiting for transfers between devices  75.3 us (44%)
  Pallas kernels  49.2 us (29%)
  blocking collectives  17 us (10%)
  starting transfers between devices  15.8 us (9%)
  local copies, waits for them, and re-layouts  12.3 us (7%)
    all_to_all x1, waiting for transfers between devices, per_device(): lax.all_to_all(send, ('mem', 'tile'), split_axis=0, concat_axis=0, tiled=...  54 us
    pallas_call x1, Pallas kernels, dispatch(): pl.pallas_call(functools.partial(dispatch_kernel, patches, capacity), out...  26.9 us
    ppermute x1, waiting for transfers between devices, per_device(): low = lax.ppermute(to_next, ('mem', 'tile'), forward)  19.3 us
    all_to_all x1, blocking collectives, per_device(): lax.all_to_all(updated.reshape(mem_count, local, cells), 'mem', split_axi...  17 us
    pallas_call x1, Pallas kernels, gram_terms(): pl.pallas_call(functools.partial(gram_kernel, mem_count, tile_count), gri...  13 us
    pallas_call x1, Pallas kernels, update(): pl.pallas_call(update_kernel, out_shape=jax.ShapeDtypeStruct(states.shape...  9.22 us
    all_to_all x1, starting transfers between devices, per_device(): lax.all_to_all(send, ('mem', 'tile'), split_axis=0, concat_axis=0, tiled=...  7.1 us
    unnamed x11, local copies, waits for them, and re-layouts  4.91 us
  transfers between devices with their start and end apart: 4, of which 3 were waited for; matrix products, arithmetic and copies ran while one was open for 1% of the time, Pallas kernels for 8%

profile of v1, /device:TPU:1, one launch (start us, length us, event | category | flops | bytes accessed | tf_op | source)
XLA Modules:
  0.0 170.3 jit_solution(308277229458625337)
XLA Ops:
  0.0 0.7 add_convert_fusion
  0.8 0.7 stack.10
  1.5 0.7 stack.9
  2.2 4.2 %concatenate.3.data_ref = bf16[144,4096]{1,0:T(8,128)(2,1)S(1)} concatenate(bf16[128,4096]{1,0:T(8,128)(2,1)} %param.7, bf16[1,4096]{1,0:T(2,128)(2,1)S(1)} %stack.9, bf16[1,4096]{1,0:T(2,128)(2,1)S(1)} %stack.10, bf16[1,4096]{1,0:T(2,128)(2,1)S(1)} %stack.11, bf16[13,4096]{1,0:T(8,128)(2,1)S(1)} %broadcast_in_dim.3), dimensions={0} | concatenate | bytes 2359296 | tf_op jit(solution)/shard_map/concatenate | solution.py:181
  6.4 0.0 copy-done.3
  6.4 26.9 %shard_map.64 = bf16[32,144,256]{2,1,0:T(8,128)(2,1)S(1)} custom-call(bf16[144,4096]{1,0:T(8,128)(2,1)S(1)} %concatenate.3.data_ref, s32[1,4096]{1,0:T(1,128)S(1)} %bitcast.15), custom_call_target="tpu_custom_call" | custom-call | tf_op jit(solution)/shard_map/pallas_call | solution.py:48
  33.3 0.0 copy-start
  33.3 1.4 copy-done
  34.7 7.1 %all-to-all-start = ((bf16[32,144,256]{2,1,0:T(8,128)(2,1)}), bf16[32,144,256]{2,1,0:T(8,128)(2,1)S(1)}, u32[]{:S(2)}, u32[]{:S(2)}) async-start(bf16[32,144,256]{2,1,0:T(8,128)(2,1)} %copy-done), calls=%async_computation | async-start | bytes 4718592 | tf_op jit(solution)/shard_map/all_to_all | solution.py:185
  41.8 0.0 copy-done.4
  41.9 1.3 copy.12
  43.1 54.0 %all-to-all-done = bf16[32,144,256]{2,1,0:T(8,128)(2,1)S(1)} async-done(((bf16[32,144,256]{2,1,0:T(8,128)(2,1)}), bf16[32,144,256]{2,1,0:T(8,128)(2,1)S(1)}, u32[]{:S(2)}, u32[]{:S(2)}) %all-to-all-start) | async-done | bytes 2359328 | tf_op jit(solution)/shard_map/all_to_all | solution.py:185
  97.2 4.3 %all-to-all-start.1 = ((bf16[4,128,1024]{2,1,0:T(8,128)(2,1)}), bf16[4,128,1024]{2,1,0:T(8,128)(2,1)S(1)}, u32[]{:S(2)}, u32[]{:S(2)}) async-start(bf16[4,128,1024]{2,1,0:T(8,128)(2,1)} %bitcast.16), calls=%async_computation.1 | async-start | bytes 2097152 | tf_op jit(solution)/shard_map/all_to_all | solution.py:183
  101.4 13.0 %shard_map.65 = (f32[528,512]{1,0:T(8,128)S(1)}, bf16[528,512]{1,0:T(8,128)(2,1)}, bf16[528,512]{1,0:T(8,128)(2,1)}) custom-call(bf16[4,8,144,256]{3,2,1,0:T(8,128)(2,1)S(1)} %bitcast.12), custom_call_target="tpu_custom_call" | custom-call | tf_op jit(solution)/shard_map/pallas_call | solution.py:104
  114.5 1.0 copy-done.1
  115.4 0.0 collective-permute-start
  115.4 4.4 %collective-permute-start.1 = (bf16[528,512]{1,0:T(8,128)(2,1)}, bf16[528,512]{1,0:T(8,128)(2,1)S(1)}, u32[]{:S(2)}, u32[]{:S(2)}) collective-permute-start(bf16[528,512]{1,0:T(8,128)(2,1)} %get-tuple-element.10), channel_id=1, source_target_pairs={{1,0},{2,1},{3,2},{4,3},{5,4},{6,5},{7,6},{8,7},{9,8},{10,9},{11,1... | collective-permute-start | bytes 1622024 | tf_op jit(solution)/shard_map/ppermute | solution.py:191
  119.9 0.0 all-to-all-done.1
  119.9 19.3 %collective-permute-done.low_ref = bf16[528,512]{1,0:T(8,128)(2,1)S(1)} collective-permute-done((bf16[528,512]{1,0:T(8,128)(2,1)}, bf16[528,512]{1,0:T(8,128)(2,1)S(1)}, u32[]{:S(2)}, u32[]{:S(2)}) %collective-permute-start) | collective-permute-done | bytes 540704 | tf_op jit(solution)/shard_map/ppermute | solution.py:190
  139.2 1.9 %collective-permute-done.1.high_ref = bf16[528,512]{1,0:T(8,128)(2,1)S(1)} collective-permute-done((bf16[528,512]{1,0:T(8,128)(2,1)}, bf16[528,512]{1,0:T(8,128)(2,1)S(1)}, u32[]{:S(2)}, u32[]{:S(2)}) %collective-permute-start.1) | collective-permute-done | bytes 540704 | tf_op jit(solution)/shard_map/ppermute | solution.py:191
  141.1 1.2 copy-done.2
  142.4 9.2 %shard_map.66 = bf16[512,1024]{1,0:T(8,128)(2,1)S(1)} custom-call(f32[528,512]{1,0:T(8,128)S(1)} %copy-done.2, bf16[528,512]{1,0:T(8,128)(2,1)S(1)} %collective-permute-done.low_ref, bf16[528,512]{1,0:T(8,128)(2,1)S(1)} %collective-permute-done.1.high_ref, bf16[512,1024]{1,0:T(8,128)(2,1)S(1)} %bitcast.13), custom_call_target="tpu_custom_call" | custom-call | tf_op jit(solution)/shard_map/pallas_call | solution.py:162
  151.6 17.0 %all_to_all.15 = bf16[4,128,1024]{2,1,0:T(8,128)(2,1)S(1)} all-to-all(bf16[4,128,1024]{2,1,0:T(8,128)(2,1)S(1)} %bitcast.14), channel_id=1, replica_groups=mesh['mem'=4,'tile'=8] {'mem'}, dimensions={0} | all-to-all | bytes 2097152 | tf_op jit(solution)/shard_map/all_to_all | solution.py:193
  168.5 1.8 %copy.10 = bf16[128,4,1,1024]{3,1,2,0:T(4,128)(2,1)} copy(bf16[128,4,1,1024]{3,0,1,2:T(8,128)(2,1)S(1)} %bitcast.17) | data formatting | bytes 2097152 | tf_op jit(solution)/shard_map/reshape | solution.py:196
  (6 shorter events, 0.0 us)
Async XLA Ops:
  0.0 6.4 %copy-start.3 = (s32[4096,1]{0,1:T(1,128)S(1)}, s32[4096,1]{0,1:T(1,128)}, u32[]{:S(2)}) copy-start(s32[4096,1]{0,1:T(1,128)} %param.10) | copy-start | bytes 49156
  33.3 1.4 copy-start
  34.7 7.1 %copy-start.4 = (bf16[128,4,1,1024]{3,1,2,0:T(4,128)(2,1)S(1)}, bf16[128,4,1,1024]{3,1,2,0:T(4,128)(2,1)}, u32[]{:S(2)}) copy-start(bf16[128,4,1,1024]{3,1,2,0:T(4,128)(2,1)} %param.6) | copy-start | bytes 3145732
  34.7 62.4 %all-to-all-start = ((bf16[32,144,256]{2,1,0:T(8,128)(2,1)}), bf16[32,144,256]{2,1,0:T(8,128)(2,1)S(1)}, u32[]{:S(2)}, u32[]{:S(2)}) async-start(bf16[32,144,256]{2,1,0:T(8,128)(2,1)} %copy-done), calls=%async_computation | async-start | bytes 4718592 | tf_op jit(solution)/shard_map/all_to_all | solution.py:185
  97.2 22.7 %all-to-all-start.1 = ((bf16[4,128,1024]{2,1,0:T(8,128)(2,1)}), bf16[4,128,1024]{2,1,0:T(8,128)(2,1)S(1)}, u32[]{:S(2)}, u32[]{:S(2)}) async-start(bf16[4,128,1024]{2,1,0:T(8,128)(2,1)} %bitcast.16), calls=%async_computation.1 | async-start | bytes 2097152 | tf_op jit(solution)/shard_map/all_to_all | solution.py:183
  114.5 1.0 copy-start.1
  115.4 23.8 %collective-permute-start = (bf16[528,512]{1,0:T(8,128)(2,1)}, bf16[528,512]{1,0:T(8,128)(2,1)S(1)}, u32[]{:S(2)}, u32[]{:S(2)}) collective-permute-start(bf16[528,512]{1,0:T(8,128)(2,1)} %get-tuple-element.9), channel_id=1, source_target_pairs={{0,1},{1,2},{2,3},{3,4},{4,5},{5,6},{6,7},{7,8},{8,9},{9,10},{10,1... | collective-permute-start | bytes 1622024 | tf_op jit(solution)/shard_map/ppermute | solution.py:190
  115.4 25.7 %collective-permute-start.1 = (bf16[528,512]{1,0:T(8,128)(2,1)}, bf16[528,512]{1,0:T(8,128)(2,1)S(1)}, u32[]{:S(2)}, u32[]{:S(2)}) collective-permute-start(bf16[528,512]{1,0:T(8,128)(2,1)} %get-tuple-element.10), channel_id=1, source_target_pairs={{1,0},{2,1},{3,2},{4,3},{5,4},{6,5},{7,6},{8,7},{9,8},{10,9},{11,1... | collective-permute-start | bytes 1622024 | tf_op jit(solution)/shard_map/ppermute | solution.py:191
  141.1 1.2 copy-start.2

commit v2 on v1

v2 whole, which is shorter than its diff:
```python
import functools
import math

import jax
import jax.numpy as jnp
from jax import lax
from jax.experimental import pallas as pl
from jax.experimental.pallas import tpu as pltpu
from jax.sharding import PartitionSpec as P

PATCH_CELLS = 128
OBS_PATCH = 1024
INFO = 16
VMEM_LIMIT = 48 * 1024 * 1024
MESH = pl.DeviceIdType.MESH
NT = (((1,), (1,)), ((), ()))


def rank_of(patches, target_ref, rank_ref):
    obs = target_ref.shape[1]
    chunk = 256
    upper = (
        lax.broadcasted_iota(jnp.int32, (chunk, chunk), 0)
        <= lax.broadcasted_iota(jnp.int32, (chunk, chunk), 1)
    ).astype(jnp.float32).astype(jnp.bfloat16)
    names = lax.broadcasted_iota(jnp.int32, (patches, chunk), 0)
    carry = jnp.zeros((patches, 1), jnp.float32)
    for start in range(0, obs, chunk):
        hit = names == target_ref[:, start : start + chunk]
        one = jnp.where(hit, 1.0, 0.0)
        run = jnp.dot(one.astype(jnp.bfloat16), upper, preferred_element_type=jnp.float32)
        rank_ref[:, start : start + chunk] = jnp.sum(one * (run + carry), 0, keepdims=True) - 1.0
        carry = carry + jnp.sum(one, 1, keepdims=True)


def add_gram(mem_count, tile_count, tile, got_ref, accs):
    local = got_ref.shape[1] - INFO
    members = local * mem_count
    values = jnp.concatenate(
        [got_ref[m * tile_count + tile][:local].astype(jnp.float32) for m in range(mem_count)], 0
    )
    info = got_ref[tile][local:].astype(jnp.float32)
    obs_mean = jnp.sum(values, 0, keepdims=True) / members
    centred = (values - obs_mean).astype(jnp.bfloat16)
    shifted = info[2:3]
    is_live = shifted > 0.5
    weight = jnp.where(is_live, 1.0 / jnp.where(is_live, info[1:2], 1.0), 0.0)
    position = shifted - 1.0
    innovation = info[0:1] - obs_mean
    first = lax.broadcasted_iota(jnp.int32, (INFO, innovation.shape[1]), 0) == 0
    vector_rows = jnp.where(first, innovation, 0.0).astype(jnp.bfloat16)
    left = jnp.concatenate([centred, vector_rows], 0)
    centred_wide = centred.astype(jnp.float32)
    for offset, acc in zip((0.0, -1.0, 1.0), accs):
        distance = (offset * PATCH_CELLS + position + 0.5 - 0.5 * PATCH_CELLS) / PATCH_CELLS
        scale = weight * jnp.exp(-2.0 * distance * distance)
        weighted = (centred_wide * scale).astype(jnp.bfloat16)
        acc[...] += lax.dot_general(left, weighted, NT, preferred_element_type=jnp.float32)


def split(a):
    high = a.astype(jnp.bfloat16)
    return high, (a - high.astype(jnp.float32)).astype(jnp.bfloat16)


def product(a, b):
    dot = functools.partial(jnp.dot, preferred_element_type=jnp.float32)
    return dot(a[0], b[0]) + (dot(a[0], b[1]) + dot(a[1], b[0]))


def transform_of(total):
    members = total.shape[1]
    diagonal = lax.broadcasted_iota(jnp.int32, (members, members), 0) == lax.broadcasted_iota(
        jnp.int32, (members, members), 1
    )
    identity = jnp.where(diagonal, 1.0, 0.0)
    gram_mat = total[:members] + (members - 1.0) * identity
    gram_vec = total[members:]
    norm_scale = jnp.sqrt(jnp.sum(gram_mat * gram_mat, keepdims=True))
    a = gram_mat / norm_scale
    a_pair = split(a)
    square = product(a_pair, a_pair)
    root = (
        2.25 * identity - 2.4375 * a + 1.6875 * square
        + product(split(square), split(0.0625 * square - 0.5625 * a))
    )
    for _ in range(2):
        root_pair = split(root)
        inner = product(a_pair, split(product(root_pair, root_pair)))
        root = 1.5 * root - 0.5 * product(root_pair, split(inner))
    inv_root = root / jnp.sqrt(norm_scale)
    inv_pair = split(inv_root)
    mean_w = product(split(product(split(gram_vec), inv_pair)), inv_pair)[:1]
    return (math.sqrt(members - 1.0) * inv_root + mean_w).astype(jnp.bfloat16)


def analysis_kernel(
    mem_count, tile_count,
    back_ref, evolved_ref, info_ref, target_ref, out_ref,
    data, rank_ref, send, got, own_acc, next_acc, prev_acc, next_send, prev_send, low, high, states, updated,
    send_sem, recv_sem, side_send, side_recv, state_send, state_recv, out_send, out_recv, own_sem,
):
    patches = mem_count * tile_count
    local, obs = evolved_ref.shape
    members = local * mem_count
    capacity = send.shape[2]
    mem, tile = lax.axis_index("mem"), lax.axis_index("tile")
    me = mem * tile_count + tile

    def device(index):
        return (lax.div(index, tile_count), lax.rem(index, tile_count))

    barrier = pltpu.get_barrier_semaphore()

    def greet(step, _):
        pl.semaphore_signal(
            barrier, inc=1, device_id=device(lax.rem(me + step, patches)), device_id_type=MESH
        )
        return 0

    lax.fori_loop(1, patches, greet, 0)
    data[:local] = evolved_ref[...]
    data[local:] = info_ref[...]
    rank_of(patches, target_ref, rank_ref)
    pl.semaphore_wait(barrier, patches - 1)

    def tile_step(index):
        return tile_count // 2 + lax.div(index + 1, 2) * (1 - 2 * lax.rem(index, 2))

    def block_copy(partner, slot):
        return pltpu.make_async_remote_copy(
            src_ref=send.at[partner], dst_ref=got.at[slot],
            send_sem=send_sem.at[partner], recv_sem=recv_sem.at[slot],
            device_id=device(partner), device_id_type=MESH,
        )

    def partner_of(step):
        to_tile = lax.rem(tile + tile_step(lax.div(step, mem_count)), tile_count)
        to_mem = lax.rem(mem + mem_count - 1 - lax.rem(step, mem_count), mem_count)
        return to_mem * tile_count + to_tile

    slots = lax.broadcasted_iota(jnp.int32, (capacity, obs), 0).astype(jnp.float32)

    def place(patch):
        rank = jnp.where(target_ref[...] == patch, rank_ref[...], -1.0)
        pick = jnp.where(slots == rank, 1.0, 0.0).astype(jnp.bfloat16)
        return lax.dot_general(data[...], pick, NT, preferred_element_type=jnp.float32).astype(jnp.bfloat16)

    def send_one(step, _):
        partner = partner_of(step)
        send[partner] = place(partner)
        block_copy(partner, me).start()
        return 0

    lax.fori_loop(0, patches - 1, send_one, 0)
    got[me] = place(me)

    def state_copy(distance):
        partner = lax.rem(mem + distance, mem_count)
        return pltpu.make_async_remote_copy(
            src_ref=back_ref.at[partner], dst_ref=states.at[mem],
            send_sem=state_send.at[distance], recv_sem=state_recv.at[distance],
            device_id=(partner, tile), device_id_type=MESH,
        )

    for distance in range(1, mem_count):
        state_copy(distance).start()
    states[mem] = back_ref[mem]

    for acc in (own_acc, next_acc, prev_acc):
        acc[...] = jnp.zeros_like(acc)
    accs = (own_acc, next_acc, prev_acc)

    def take_tile(index, _):
        source_tile = lax.rem(tile + tile_count - tile_step(index), tile_count)
        for m in range(mem_count):
            source = m * tile_count + source_tile
            block_copy(source, source).wait_recv()
        add_gram(mem_count, tile_count, source_tile, got, accs)
        return 0

    lax.fori_loop(0, tile_count - 1, take_tile, 0)
    for distance in range(1, mem_count):
        source = lax.rem(mem + distance, mem_count) * tile_count + tile
        block_copy(source, source).wait_recv()
    add_gram(mem_count, tile_count, tile, got, accs)

    next_send[...] = next_acc[...].astype(jnp.bfloat16)
    prev_send[...] = prev_acc[...].astype(jnp.bfloat16)

    def side_copy(block, target, which, distance):
        return pltpu.make_async_remote_copy(
            src_ref=block, dst_ref=target,
            send_sem=side_send.at[which], recv_sem=side_recv.at[which],
            device_id=device(lax.rem(me + distance, patches)), device_id_type=MESH,
        )

    sides = (side_copy(next_send, low, 0, 1), side_copy(prev_send, high, 1, patches - 1))
    for side in sides:
        side.start()

    for distance in range(1, mem_count):
        state_copy(distance).wait()
    wide = states[...].reshape(members, states.shape[2]).astype(jnp.float32)
    state_mean = jnp.sum(wide, 0, keepdims=True) / members
    deviation = (wide - state_mean).astype(jnp.bfloat16)
    for side in sides:
        side.wait()
    total = own_acc[...] + low[...].astype(jnp.float32) + high[...].astype(jnp.float32)
    transform = transform_of(total)
    mixed = jnp.dot(transform, deviation, preferred_element_type=jnp.float32)
    updated[...] = (state_mean + mixed).astype(jnp.bfloat16).reshape(updated.shape)

    def out_copy(distance):
        partner = lax.rem(mem + distance, mem_count)
        return pltpu.make_async_remote_copy(
            src_ref=updated.at[partner], dst_ref=out_ref.at[mem],
            send_sem=out_send.at[distance], recv_sem=out_recv.at[distance],
            device_id=(partner, tile), device_id_type=MESH,
        )

    for distance in range(1, mem_count):
        out_copy(distance).start()
    mine = pltpu.make_async_copy(updated.at[mem], out_ref.at[mem], own_sem)
    mine.start()
    mine.wait()
    for distance in range(1, mem_count):
        out_copy(distance).wait()

    def finish(step, _):
        block_copy(partner_of(step), me).wait_send()
        return 0

    lax.fori_loop(0, patches - 1, finish, 0)


def per_device(background, evolved, obs_value, obs_var, obs_patch, obs_pos):
    mem_count = lax.axis_size("mem")
    tile_count = lax.axis_size("tile")
    patches = mem_count * tile_count
    local, obs = evolved.shape
    members = local * mem_count
    cells = background.shape[3]
    capacity = 2 * OBS_PATCH // tile_count
    info = jnp.stack([obs_value, obs_var, (obs_pos + 1).astype(jnp.bfloat16)])
    info = jnp.concatenate([info, jnp.zeros((INFO - 3, obs), jnp.bfloat16)], 0)
    states = background[:, :, 0, :].transpose(1, 0, 2)
    rows = local + INFO
    gram_shape = (members + INFO, members)
    dma = pltpu.SemaphoreType.DMA
    analysis = pl.pallas_call(
        functools.partial(analysis_kernel, mem_count, tile_count),
        out_shape=jax.ShapeDtypeStruct((mem_count, local, cells), jnp.bfloat16),
        in_specs=[pl.BlockSpec(memory_space=pltpu.VMEM)] * 4,
        out_specs=pl.BlockSpec(memory_space=pl.ANY),
        scratch_shapes=[
            pltpu.VMEM((rows, obs), jnp.bfloat16),
            pltpu.VMEM((1, obs), jnp.float32),
            pltpu.VMEM((patches, rows, capacity), jnp.bfloat16),
            pltpu.VMEM((patches, rows, capacity), jnp.bfloat16),
            *[pltpu.VMEM(gram_shape, jnp.float32)] * 3,
            *[pltpu.VMEM(gram_shape, jnp.bfloat16)] * 4,
            *[pltpu.VMEM((mem_count, local, cells), jnp.bfloat16)] * 2,
            dma((patches,)),
            dma((patches,)),
            dma((2,)),
            dma((2,)),
            *[dma((mem_count,))] * 4,
            dma(()),
        ],
        compiler_params=pltpu.CompilerParams(
            collective_id=0, has_side_effects=True, vmem_limit_bytes=VMEM_LIMIT
        ),
    )(states, evolved, info, obs_patch.reshape(1, obs))
    return analysis.transpose(1, 0, 2).reshape(background.shape)


def solution(mesh):
    return jax.shard_map(
        per_device,
        mesh=mesh,
        in_specs=(
            P("mem", None, "tile", None),
            P("mem", "tile"),
            P("tile"),
            P("tile"),
            P("tile", None),
            P("tile"),
        ),
        out_specs=P("mem", None, "tile", None),
        check_vma=False,
    )
```

time: 172 us -> 117 us (0.68); the launches traced: 170 us -> 117 us
  waiting for transfers between devices: 75.3 us -> 0 us
  Pallas kernels: 49.2 us -> 111 us
  blocking collectives: 17 us -> 0 us
  starting transfers between devices: 15.8 us -> 0 us
  local copies, waits for them, and re-layouts: 12.3 us -> 4.89 us
    pallas_call x3 -> x1, Pallas kernels: 49.2 us -> 111 us  [per_device(): pl.pallas_call(functools.partial(analysis_kernel, mem_count, tile_count),...]
    all_to_all x2 -> x0, waiting for transfers between devices: 54 us -> none  [the longest x1 54 us: per_device(): lax.all_to_all(send, ('mem', 'tile'), split_axis=0, concat_axis=0, tiled=...]
    ppermute x2 -> x0, waiting for transfers between devices: 21.2 us -> none  [the longest x1 19.3 us: per_device(): low = lax.ppermute(to_next, ('mem', 'tile'), forward)]
    all_to_all x1 -> x0, blocking collectives: 17 us -> none  [per_device(): lax.all_to_all(updated.reshape(mem_count, local, cells), 'mem', split_axi...]
    all_to_all x2 -> x0, starting transfers between devices: 11.4 us -> none  [the longest x1 7.1 us: per_device(): lax.all_to_all(send, ('mem', 'tile'), split_axis=0, concat_axis=0, tiled=...]
    ppermute x2 -> x0, starting transfers between devices: 4.44 us -> none  [the longest x1 4.44 us: per_device(): high = lax.ppermute(to_prev, ('mem', 'tile'), backward)]
    concatenate x1, local copies, waits for them, and re-layouts: 4.2 us -> 0.08 us  [per_device(): info = jnp.concatenate([info, jnp.zeros((INFO - 3, obs), jnp.bfloat16)], 0)]
    unnamed x11 -> x9, local copies, waits for them, and re-layouts: 4.91 us -> 3 us
  transfers between devices with their start and end apart: 4 -> 0, of which waited for: 3 -> 0; matrix products, arithmetic and copies ran while one was open for 1% -> 0% of each run, Pallas kernels for 8% -> 0%
where the time goes in v2:
time: 117 us
  Pallas kernels  111 us (95%)
  local copies, waits for them, and re-layouts  4.89 us (4%)
    pallas_call x1, Pallas kernels, per_device(): pl.pallas_call(functools.partial(analysis_kernel, mem_count, tile_count),...  111 us
    unnamed x9, local copies, waits for them, and re-layouts  3 us

profile of v2, /device:TPU:1, one launch (start us, length us, event | category | flops | bytes accessed | tf_op | source)
XLA Modules:
  0.0 117.1 jit_solution(6733425775034525535)
XLA Ops:
  0.0 0.1 pad.3.clone
  0.1 0.7 add_convert_fusion
  0.8 0.0 copy-start.2
  0.8 0.7 copy-done.2
  1.5 0.0 copy-start.3
  1.5 0.7 copy-done.3
  2.2 0.1 maximum_maximum_fusion.info_ref
  2.3 0.0 copy-start
  2.3 0.0 copy-start.1
  2.3 1.6 %copy.10 = bf16[128,4,1,1024]{3,0,1,2:T(8,128)(2,1)S(1)} copy(bf16[128,4,1,1024]{3,1,2,0:T(4,128)(2,1)} %param.6) | data formatting | bytes 2097152 | tf_op args[0]
  4.0 0.0 copy-done
  4.0 0.0 copy-done.1
  4.0 111.4 %shard_map.64 = bf16[4,128,1024]{2,1,0:T(8,128)(2,1)S(1)} custom-call(bf16[4,128,1024]{2,1,0:T(8,128)(2,1)S(1)} %bitcast.10, bf16[128,4096]{1,0:T(8,128)(2,1)S(1)} %copy-done, bf16[16,4096]{1,0:T(8,128)(2,1)S(1)} %maximum_maximum_fusion.info_ref, s32[1,4096]{1,0:T(1,128)S(1)} %bitcast.11), custom_call_target="tpu_custom_call" | custom-call | tf_op jit(solution)/shard_map/pallas_call | solution.py:251
  115.4 1.8 %copy.8 = bf16[128,4,1,1024]{3,1,2,0:T(4,128)(2,1)} copy(bf16[128,4,1,1024]{3,0,1,2:T(8,128)(2,1)S(1)} %bitcast.9) | data formatting | bytes 2097152 | tf_op jit(solution)/shard_map/reshape | solution.py:275
  (4 shorter events, 0.0 us)
Async XLA Ops:
  0.8 0.7 copy-start.2
  1.5 0.7 copy-start.3
  2.3 1.7 %copy-start = (bf16[128,4096]{1,0:T(8,128)(2,1)S(1)}, bf16[128,4096]{1,0:T(8,128)(2,1)}, u32[]{:S(2)}) copy-start(bf16[128,4096]{1,0:T(8,128)(2,1)} %evolved_ref.1) | copy-start | bytes 3145732
  2.3 1.7 %copy-start.1 = (s32[4096,1]{0,1:T(1,128)S(1)}, s32[4096,1]{0,1:T(1,128)}, u32[]{:S(2)}) copy-start(s32[4096,1]{0,1:T(1,128)} %param.10) | copy-start | bytes 49156

commit v3 on v2

--- a/solution.py
+++ b/solution.py
@@ -195,7 +195,15 @@
             device_id=device(lax.rem(me + distance, patches)), device_id_type=MESH,
         )
 
-    sides = (side_copy(next_send, low, 0, 1), side_copy(prev_send, high, 1, patches - 1))
+    half = members // 2
+    parts = ((pl.ds(half, half + INFO), pl.ds(0, members)), (pl.ds(0, half), pl.ds(0, half)))
+    sides = [
+        side_copy(block.at[part], target.at[part], 2 * k + side, distance)
+        for k, part in enumerate(parts)
+        for side, (block, target, distance) in enumerate(
+            ((next_send, low, 1), (prev_send, high, patches - 1))
+        )
+    ]
     for side in sides:
         side.start()
 
@@ -206,7 +214,9 @@
     deviation = (wide - state_mean).astype(jnp.bfloat16)
     for side in sides:
         side.wait()
-    total = own_acc[...] + low[...].astype(jnp.float32) + high[...].astype(jnp.float32)
+    below, top = [low[part].astype(jnp.float32) + high[part].astype(jnp.float32) for part in parts]
+    side_sum = jnp.concatenate([jnp.concatenate([top, below[:half, :half].T], 1), below], 0)
+    total = own_acc[...] + side_sum
     transform = transform_of(total)
     mixed = jnp.dot(transform, deviation, preferred_element_type=jnp.float32)
     updated[...] = (state_mean + mixed).astype(jnp.bfloat16).reshape(updated.shape)
@@ -263,8 +273,8 @@
             *[pltpu.VMEM((mem_count, local, cells), jnp.bfloat16)] * 2,
             dma((patches,)),
             dma((patches,)),
-            dma((2,)),
-            dma((2,)),
+            dma((4,)),
+            dma((4,)),
             *[dma((mem_count,))] * 4,
             dma(()),
         ],

time: 117 us -> 112 us (0.957)
  Pallas kernels: 111 us -> 106 us
    pallas_call x1, Pallas kernels: 111 us -> 106 us  [per_device(): pl.pallas_call(functools.partial(analysis_kernel, mem_count, tile_count),...]
where the time goes in v3:
time: 112 us; the launch traced here: 111 us
  Pallas kernels  106 us (95%)
  local copies, waits for them, and re-layouts  4.89 us (4%)
    pallas_call x1, Pallas kernels, per_device(): pl.pallas_call(functools.partial(analysis_kernel, mem_count, tile_count),...  106 us
    unnamed x9, local copies, waits for them, and re-layouts  3 us

profile of v3, /device:TPU:1, one launch (start us, length us, event | category | flops | bytes accessed | tf_op | source)
XLA Modules:
  0.0 111.5 jit_solution(1044235340594194954)
XLA Ops:
  0.0 0.1 pad.3.clone
  0.1 0.7 add_convert_fusion
  0.8 0.0 copy-start.2
  0.8 0.7 copy-done.2
  1.5 0.0 copy-start.3
  1.5 0.7 copy-done.3
  2.2 0.1 maximum_maximum_fusion.info_ref
  2.3 0.0 copy-start
  2.3 0.0 copy-start.1
  2.3 1.6 %copy.10 = bf16[128,4,1,1024]{3,0,1,2:T(8,128)(2,1)S(1)} copy(bf16[128,4,1,1024]{3,1,2,0:T(4,128)(2,1)} %param.6) | data formatting | bytes 2097152 | tf_op args[0]
  4.0 0.0 copy-done
  4.0 0.0 copy-done.1
  4.0 105.7 %shard_map.64 = bf16[4,128,1024]{2,1,0:T(8,128)(2,1)S(1)} custom-call(bf16[4,128,1024]{2,1,0:T(8,128)(2,1)S(1)} %bitcast.10, bf16[128,4096]{1,0:T(8,128)(2,1)S(1)} %copy-done, bf16[16,4096]{1,0:T(8,128)(2,1)S(1)} %maximum_maximum_fusion.info_ref, s32[1,4096]{1,0:T(1,128)S(1)} %bitcast.11), custom_call_target="tpu_custom_call" | custom-call | tf_op jit(solution)/shard_map/pallas_call | solution.py:261
  109.7 1.8 %copy.8 = bf16[128,4,1,1024]{3,1,2,0:T(4,128)(2,1)} copy(bf16[128,4,1,1024]{3,0,1,2:T(8,128)(2,1)S(1)} %bitcast.9) | data formatting | bytes 2097152 | tf_op jit(solution)/shard_map/reshape | solution.py:285
  (4 shorter events, 0.0 us)
Async XLA Ops:
  0.8 0.7 copy-start.2
  1.5 0.7 copy-start.3
  2.3 1.7 %copy-start = (bf16[128,4096]{1,0:T(8,128)(2,1)S(1)}, bf16[128,4096]{1,0:T(8,128)(2,1)}, u32[]{:S(2)}) copy-start(bf16[128,4096]{1,0:T(8,128)(2,1)} %evolved_ref.1) | copy-start | bytes 3145732
  2.3 1.7 %copy-start.1 = (s32[4096,1]{0,1:T(1,128)S(1)}, s32[4096,1]{0,1:T(1,128)}, u32[]{:S(2)}) copy-start(s32[4096,1]{0,1:T(1,128)} %param.10) | copy-start | bytes 49156
